TPU v7x, 512 devices: a whole 4x4x16 slice. The times are simulated.
512 devices in a mesh: row: 32 (over x, y, core), col: 16 (over z).
Axes of the slice: x: 4, y: 4, z: 16, core: 2. Of those that a mesh axis runs over, the one named last changes fastest.
Arguments:
- descriptors: bfloat16 [32, 98304], P(None, ('row', 'col')), may hold values from -6 to 6
- densities: float32 [98304], P(('row', 'col')), may hold values from 0.25 to 4
- vectors: float32 [32, 98304], P(None, ('row', 'col')), may hold values from -6 to 6
Outputs:
- next_block: float32 [32, 98304], P(None, ('row', 'col'))
All inputs are finite; a program needn't handle non-finite values.
Results may differ from a plain program's by a relative error of at most 0.0036.
Values may be sent and summed in bfloat16 or wider, within the bound.
A program may use at most 64 MiB of HBM per device.

v0:
```python
import math
import jax
import jax.numpy as jnp
from jax import lax
from jax.sharding import Mesh
from jax.sharding import PartitionSpec as P

ROW = ("row_0", "row_1", "row_2")
ROW_COL = ("row_0", "row_1", "row_2", "col")
kernel_width = 8.0


def from_everyone(shard, axis):
    count = lax.axis_size(axis)
    return lax.all_to_all(
        jnp.broadcast_to(shard[None], (count, *shard.shape)), axis, 0, 0, tiled=True
    )


def laid_out(tiles, dim):
    shape = list(tiles.shape[1:])
    shape[dim] *= tiles.shape[0]
    return jnp.moveaxis(tiles, 0, dim).reshape(shape)


def gather_directly(shard, axis, dim):
    tiles = from_everyone(shard, axis)
    return laid_out(tiles, dim)


def turned_gather(arrays, axis, dims):
    turned = [jnp.moveaxis(a, dim, 0) for a, dim in zip(arrays, dims)]
    widths = [t[0].size for t in turned]
    both = jnp.concatenate([t.reshape(-1, w) for t, w in zip(turned, widths)], axis=1)
    filled = lax.all_gather(both, axis, axis=0, tiled=True)
    tiles = jnp.split(filled, [sum(widths[:k]) for k in range(1, len(widths))], axis=1)
    return tuple(
        (
            jnp.moveaxis(b.reshape(-1, *t.shape[1:]), 0, dim)
            for b, t, dim in zip(tiles, turned, dims)
        )
    )


def cut_along(shard, dim, count):
    before, after = (shard.shape[:dim], shard.shape[dim + 1 :])
    return jnp.moveaxis(shard.reshape(*before, count, -1, *after), dim, 0)


def sent_and_summed(shard, axis, dim):
    count = lax.axis_size(axis)
    tiles = lax.all_to_all(cut_along(shard, dim, count), axis, 0, 0, tiled=True)
    return jnp.sum(tiles, axis=0)


def side_by_side(arrays, axis, dim, along):
    ends, at = ([], 0)
    for a in arrays[:-1]:
        at += a.shape[along]
        ends.append(at)
    both = jnp.concatenate(arrays, axis=along)
    return tuple(jnp.split(sent_and_summed(both, axis, dim), ends, axis=along))


def over_copies(shard, axis):
    return from_everyone(shard, axis).sum(axis=0)


def one_axis_at_a_time(shard, axes):
    far, near = axes
    return over_copies(over_copies(shard, near), far)


def in_one(arrays, axis):
    flat, at, finished = (jnp.concatenate([a.reshape(-1) for a in arrays]), 0, [])
    running = one_axis_at_a_time(flat, axis)
    for a in arrays:
        finished.append(running[at : at + a.size].reshape(a.shape))
        at += a.size
    return tuple(finished)


def tile_terms(targets, target_norm, piece):
    piece_feat, piece_vals, piece_inv = piece
    piece_norm = jnp.sum(jnp.square(piece_feat.astype(jnp.float32)), axis=0)
    feature_dim, target_count = targets.shape
    span_rows = math.gcd(target_count, 512)
    block_count = target_count // span_rows
    blocks = targets.reshape(feature_dim, block_count, span_rows).transpose(1, 0, 2)
    norm_blocks = target_norm.reshape(block_count, span_rows)

    def tile_block(block_item):
        block_feat, block_norm = block_item
        inner_prod = lax.dot_general(
            block_feat, piece_feat, (((0,), (0,)), ((), ())), preferred_element_type=jnp.float32
        )
        kernel = jnp.exp(
            -(block_norm[:, None] + piece_norm[None, :] - 2.0 * inner_prod) / kernel_width
        ).astype(jnp.bfloat16)
        numerator = lax.dot_general(
            piece_vals, kernel, (((1,), (1,)), ((), ())), preferred_element_type=jnp.float32
        )
        degree = lax.dot_general(
            piece_inv, kernel, (((1,), (1,)), ((), ())), preferred_element_type=jnp.float32
        )
        return (numerator, degree)

    numerator, degree = lax.map(tile_block, (blocks, norm_blocks))
    numerator = numerator.transpose(1, 0, 2).reshape(piece_vals.shape[0], target_count)
    degree = degree.transpose(1, 0, 2).reshape(1, target_count)
    return (numerator, degree)


def accumulate(targets, vec_count):
    target_norm = jnp.sum(jnp.square(targets.astype(jnp.float32)), axis=0)

    def fold_piece(running, piece, start):
        numerator, degree = tile_terms(targets, target_norm, piece)
        return (numerator, degree)

    initial = (
        jnp.zeros((vec_count, targets.shape[1]), jnp.float32),
        jnp.zeros((1, targets.shape[1]), jnp.float32),
    )
    return (fold_piece, initial)


def per_device(descriptors, densities, vectors):
    highest = lax.Precision.HIGHEST
    vec_count = vectors.shape[0]
    weighted = (vectors / densities[None, :]).astype(jnp.bfloat16)
    inverse = (1.0 / densities).astype(jnp.bfloat16)[None, :]
    targets = gather_directly(descriptors, ROW, 1)
    fold_piece, initial = accumulate(targets, vec_count)
    partial_value = fold_piece(
        initial, turned_gather((descriptors, weighted, inverse), "col", (1, 1, 1)), jnp.int32(0)
    )
    numerator, degree = side_by_side((partial_value[0], partial_value[1]), ROW, 1, 0)
    diffused = numerator / degree
    samples_float = float(descriptors.shape[1] * lax.axis_size(ROW) * lax.axis_size("col"))
    coupling, diffused_gram, basis_gram = in_one(
        (
            jnp.dot(vectors, diffused.T, precision=highest),
            jnp.dot(diffused, diffused.T, precision=highest),
            jnp.dot(vectors, vectors.T, precision=highest),
        ),
        (("row_0", "row_1"), ("row_2", "col")),
    )
    remainder = diffused - jnp.dot(coupling.T, vectors, precision=highest) / samples_float
    cross_term = jnp.dot(coupling.T, coupling, precision=highest)
    basis_term = jnp.dot(
        coupling.T, jnp.dot(basis_gram, coupling, precision=highest), precision=highest
    )
    spread = (
        diffused_gram
        - 2.0 * cross_term / samples_float
        + basis_term / (samples_float * samples_float)
    )
    factor = jnp.linalg.cholesky(spread)
    solved = jax.scipy.linalg.solve_triangular(factor, remainder, lower=True)
    return math.sqrt(samples_float) * solved


def solution(mesh):
    finer = Mesh(
        mesh.devices.reshape(4, 4, 2, mesh.shape["col"]), ("row_0", "row_1", "row_2", "col")
    )
    placed = (P(None, ROW_COL), P(ROW_COL), P(None, ROW_COL))
    return jax.shard_map(
        per_device, mesh=finer, in_specs=placed, out_specs=P(None, ROW_COL), check_vma=False
    )
```

profile of v0, /device:TPU:1, one launch (start us, length us, event | category | flops | bytes accessed | tf_op | source)
XLA Modules:
  0.0 182.3 jit_solution(6465203450939220424)
XLA Ops:
  0.0 1.6 broadcast_in_dim.23
  1.6 10.4 %all-to-all-start = ((bf16[32,32,192]{2,1,0:T(8,128)(2,1)}), bf16[32,32,192]{2,1,0:T(8,128)(2,1)S(1)}, u32[]{:S(2)}, u32[]{:S(2)}) async-start(bf16[32,32,192]{2,1,0:T(8,128)(2,1)} %broadcast_in_dim.23), calls=%async_computation | async-start | bytes 1048576 | tf_op jit(solution)/shard_map/all_to_all | solution.py:15
  14.2 29.9 %all-gather = bf16[16,192,65]{1,2,0:T(8,128)(2,1)S(1)} all-gather(bf16[1,192,65]{1,2,0:T(8,128)(2,1)S(1)} %maximum_bitcast_fusion.1), channel_id=1, replica_groups=mesh['row_0'=4,'row_1'=4,'row_2'=2,'col'=16] {'col'}, dimensions={0}, use_global_device_ids=true | all-gather | bytes 424320 | tf_op jit(solution)/shard_map/all_gather | solution.py:35
  46.5 43.8 %while.12 = (s32[]{:T(128)}, f32[12,32,512]{2,1,0:T(8,128)S(1)}, f32[12,1,512]{2,1,0:T(1,128)S(1)}, f32[12,512]{1,0:T(8,128)S(1)}, f32[3072]{0:T(1024)S(1)}, /*i...) while((s32[]{:T(128)}, f32[12,32,512]{2,1,0:T(8,128)S(1)}, ...), condition=%wide.region_3.4_spmd, body=%wide.region_2.3_spmd.sunk | while | flops 213909504 | bytes 9961589 | solution.py:108
  46.5 1.7 exponential_convert_fusion.2
  50.1 1.7 exponential_convert_fusion.2
  51.8 1.0 fusion.47
  53.8 1.7 exponential_convert_fusion.2
  57.5 1.7 exponential_convert_fusion.2
  61.1 1.7 exponential_convert_fusion.2
  64.8 1.7 exponential_convert_fusion.2
  68.4 1.7 exponential_convert_fusion.2
  72.1 1.7 exponential_convert_fusion.2
  75.7 1.7 exponential_convert_fusion.2
  79.4 1.7 exponential_convert_fusion.2
  83.0 1.7 exponential_convert_fusion.2
  86.7 1.7 exponential_convert_fusion.2
  91.6 1.7 copy.49
  93.3 14.3 %all-to-all-start.1 = ((f32[32,33,192]{2,1,0:T(8,128)}), f32[32,33,192]{2,1,0:T(8,128)S(1)}, u32[]{:S(2)}, u32[]{:S(2)}) async-start(f32[32,33,192]{2,1,0:T(8,128)} %copy.49), calls=%async_computation.1 | async-start | bytes 2621440 | tf_op jit(solution)/shard_map/all_to_all | solution.py:52
  107.9 19.5 %all-to-all-done.1 = f32[32,33,192]{2,1,0:T(8,128)S(1)} async-done(((f32[32,33,192]{2,1,0:T(8,128)}), f32[32,33,192]{2,1,0:T(8,128)S(1)}, u32[]{:S(2)}, u32[]{:S(2)}) %all-to-all-start.1) | async-done | bytes 811040 | tf_op jit(solution)/shard_map/all_to_all | solution.py:52
  128.3 33.9 %all_to_all.22 = f32[32,1,3072]{2,1,0:T(1,128)S(1)} all-to-all(f32[32,1,3072]{2,1,0:T(1,128)S(1)} %broadcast_in_dim.40), channel_id=1, replica_groups=mesh['row_0'=4,'row_1'=4,'row_2'=2,'col'=16] {'row_2','col'}, dimensions={0} | all-to-all | bytes 786432 | tf_op jit(solution)/shard_map/all_to_all | solution.py:15
  162.5 10.9 %all_to_all.23 = f32[16,1,3072]{2,1,0:T(1,128)S(1)} all-to-all(f32[16,1,3072]{2,1,0:T(1,128)S(1)} %broadcast_in_dim.41), channel_id=1, replica_groups=mesh['row_0'=4,'row_1'=4,'row_2'=2,'col'=16] {'row_0','row_1'}, dimensions={0} | all-to-all | bytes 393216 | tf_op jit(solution)/shard_map/all_to_all | solution.py:15
  174.8 2.9 %cholesky.16 = f32[32,32]{1,0:T(8,128)S(1)} custom-call(f32[32,32]{1,0:T(8,128)S(1)} %fusion.11), custom_call_target="Cholesky" | custom-call | tf_op jit(solution)/shard_map/jit(cholesky)/cholesky | solution.py:159
  179.0 2.4 %custom-call.7 = f32[1,32,32]{1,2,0:T(8,128)S(1)} custom-call(f32[1,32,32]{2,1,0:T(8,128)S(1)} %fusion.9), custom_call_target="InvertDiagBlocksLowerTriangular" | custom-call | tf_op jit(solution)/shard_map/jit(_solve_triangular)/triangular_solve | solution.py:160
  (88 shorter events, 33.4 us)
Async XLA Ops:
  1.6 43.4 %all-to-all-start = ((bf16[32,32,192]{2,1,0:T(8,128)(2,1)}), bf16[32,32,192]{2,1,0:T(8,128)(2,1)S(1)}, u32[]{:S(2)}, u32[]{:S(2)}) async-start(bf16[32,32,192]{2,1,0:T(8,128)(2,1)} %broadcast_in_dim.23), calls=%async_computation | async-start | bytes 1048576 | tf_op jit(solution)/shard_map/all_to_all | solution.py:15
  91.5 16.1 %copy-start = (f32[32,192]{1,0:T(8,128)S(1)}, f32[32,192]{1,0:T(8,128)}, u32[]{:S(2)}) copy-start(f32[32,192]{1,0:T(8,128)} %param.7) | copy-start | bytes 73732
  93.3 34.1 %all-to-all-start.1 = ((f32[32,33,192]{2,1,0:T(8,128)}), f32[32,33,192]{2,1,0:T(8,128)S(1)}, u32[]{:S(2)}, u32[]{:S(2)}) async-start(f32[32,33,192]{2,1,0:T(8,128)} %copy.49), calls=%async_computation.1 | async-start | bytes 2621440 | tf_op jit(solution)/shard_map/all_to_all | solution.py:52
where the time goes:
time: 183 us; the launch traced here: 182 us
  blocking collectives  74.7 us (41%)
  matrix products  45.7 us (25%)
  starting transfers between devices  24.7 us (13%)
  waiting for transfers between devices  19.5 us (11%)
  other arithmetic  9.74 us (5%)
  local copies, waits for them, and re-layouts  7.53 us (4%)
    all_to_all x2, blocking collectives, from_everyone(): lax.all_to_all(jnp.broadcast_to(shard[None], (count, *shard.shape)), axis...  44.8 us
    all_gather x1, blocking collectives, turned_gather(): filled = lax.all_gather(both, axis, axis=0, tiled=True)  29.9 us
    dot_general x12, matrix products, tile_block(): lax.dot_general(block_feat, piece_feat, (((0,), (0,)), ((), ())), preferr...  19.9 us
    all_to_all x1, waiting for transfers between devices, sent_and_summed(): tiles = lax.all_to_all(cut_along(shard, dim, count), axis, 0, 0, tiled=True)  19.5 us
    all_to_all x1, starting transfers between devices, sent_and_summed(): tiles = lax.all_to_all(cut_along(shard, dim, count), axis, 0, 0, tiled=True)  14.3 us
    dot_general x12, matrix products, tile_block(): lax.dot_general(piece_vals, kernel, (((1,), (1,)), ((), ())), preferred_e...  12.5 us
    dot_general x12, matrix products, tile_block(): lax.dot_general(piece_inv, kernel, (((1,), (1,)), ((), ())), preferred_el...  11.2 us
    all_to_all x1, starting transfers between devices, from_everyone(): lax.all_to_all(jnp.broadcast_to(shard[None], (count, *shard.shape)), axis...  10.4 us
  transfers between devices with their start and end apart: 2, of which 1 were waited for; matrix products, arithmetic and copies ran while one was open for 2% of the time, Pallas kernels for 0%

commit v1 on v0

--- a/solution.py
+++ b/solution.py
@@ -32,7 +32,10 @@
     turned = [jnp.moveaxis(a, dim, 0) for a, dim in zip(arrays, dims)]
     widths = [t[0].size for t in turned]
     both = jnp.concatenate([t.reshape(-1, w) for t, w in zip(turned, widths)], axis=1)
-    filled = lax.all_gather(both, axis, axis=0, tiled=True)
+    frames = []
+    for _ in range(lax.axis_size(axis)):
+        frames.append(both)
+    filled = jnp.concatenate(lax.all_to_all(jnp.stack(frames, 0), axis, 0, 0), 0)
     tiles = jnp.split(filled, [sum(widths[:k]) for k in range(1, len(widths))], axis=1)
     return tuple(
         (

time: 183 us -> 196 us (1.071)
  waiting for transfers between devices: 19.5 us -> 55.7 us
  blocking collectives: 74.7 us -> 43.8 us
  starting transfers between devices: 24.7 us -> 31.9 us
    all_gather x1 -> x0, blocking collectives: 29.9 us -> none  [turned_gather(): filled = lax.all_gather(both, axis, axis=0, tiled=True)]
    all_to_all x0 -> x1, waiting for transfers between devices: none -> 26.6 us  [turned_gather(): lax.all_to_all(jnp.stack(frames, 0), axis, 0, 0)]
    all_to_all x0 -> x1, starting transfers between devices: none -> 13 us  [turned_gather(): lax.all_to_all(jnp.stack(frames, 0), axis, 0, 0)]
    all_to_all x1, waiting for transfers between devices: 0.01 us -> 9.54 us  [from_everyone(): lax.all_to_all(jnp.broadcast_to(shard[None], (count, *shard.shape)), axis...]
    all_to_all x1, starting transfers between devices: 14.3 us -> 8.53 us  [sent_and_summed(): tiles = lax.all_to_all(cut_along(shard, dim, count), axis, 0, 0, tiled=True)]
  transfers between devices with their start and end apart: 2 -> 3, of which waited for: 1 -> 3; matrix products, arithmetic and copies ran while one was open for 2% -> 2% of each run, Pallas kernels for 0% -> 0%
where the time goes in v1:
time: 196 us
  waiting for transfers between devices  55.7 us (28%)
  matrix products  45.7 us (23%)
  blocking collectives  43.8 us (22%)
  starting transfers between devices  31.9 us (16%)
  other arithmetic  9.74 us (5%)
  local copies, waits for them, and re-layouts  8.38 us (4%)
    all_to_all x2, blocking collectives, from_everyone(): lax.all_to_all(jnp.broadcast_to(shard[None], (count, *shard.shape)), axis...  43.8 us
    all_to_all x1, waiting for transfers between devices, turned_gather(): lax.all_to_all(jnp.stack(frames, 0), axis, 0, 0)  26.6 us
    dot_general x12, matrix products, tile_block(): lax.dot_general(block_feat, piece_feat, (((0,), (0,)), ((), ())), preferr...  19.9 us
    all_to_all x1, waiting for transfers between devices, sent_and_summed(): tiles = lax.all_to_all(cut_along(shard, dim, count), axis, 0, 0, tiled=True)  19.6 us
    all_to_all x1, starting transfers between devices, turned_gather(): lax.all_to_all(jnp.stack(frames, 0), axis, 0, 0)  13 us
    dot_general x12, matrix products, tile_block(): lax.dot_general(piece_vals, kernel, (((1,), (1,)), ((), ())), preferred_e...  12.5 us
    dot_general x12, matrix products, tile_block(): lax.dot_general(piece_inv, kernel, (((1,), (1,)), ((), ())), preferred_el...  11.2 us
    all_to_all x1, starting transfers between devices, from_everyone(): lax.all_to_all(jnp.broadcast_to(shard[None], (count, *shard.shape)), axis...  10.4 us
  transfers between devices with their start and end apart: 3, of which 3 were waited for; matrix products, arithmetic and copies ran while one was open for 2% of the time, Pallas kernels for 0%

profile of v1, /device:TPU:1, one launch (start us, length us, event | category | flops | bytes accessed | tf_op | source)
XLA Modules:
  0.0 195.7 jit_solution(6593952178241605016)
XLA Ops:
  1.6 10.4 %all-to-all-start = ((bf16[32,32,192]{2,1,0:T(8,128)(2,1)}), bf16[32,32,192]{2,1,0:T(8,128)(2,1)S(1)}, u32[]{:S(2)}, u32[]{:S(2)}) async-start(bf16[32,32,192]{2,1,0:T(8,128)(2,1)} %broadcast_in_dim.23), calls=%async_computation | async-start | bytes 1048576 | tf_op jit(solution)/shard_map/all_to_all | solution.py:15
  14.2 9.5 %all-to-all-done = bf16[32,32,192]{2,1,0:T(8,128)(2,1)S(1)} async-done(((bf16[32,32,192]{2,1,0:T(8,128)(2,1)}), bf16[32,32,192]{2,1,0:T(8,128)(2,1)S(1)}, u32[]{:S(2)}, u32[]{:S(2)}) %all-to-all-start) | async-done | bytes 393248 | tf_op jit(solution)/shard_map/all_to_all | solution.py:15
  24.6 13.0 %all-to-all-start.1 = ((bf16[16,192,65]{1,2,0:T(8,128)(2,1)}), bf16[16,192,65]{1,2,0:T(8,128)(2,1)S(1)}, u32[]{:S(2)}, u32[]{:S(2)}) async-start(bf16[16,192,65]{1,2,0:T(8,128)(2,1)} %stack.2), calls=%async_computation.1 | async-start | bytes 1179648 | tf_op jit(solution)/shard_map/all_to_all | solution.py:38
  39.1 26.6 %all-to-all-done.1 = bf16[16,192,65]{1,2,0:T(8,128)(2,1)S(1)} async-done(((bf16[16,192,65]{1,2,0:T(8,128)(2,1)}), bf16[16,192,65]{1,2,0:T(8,128)(2,1)S(1)}, u32[]{:S(2)}, u32[]{:S(2)}) %all-to-all-start.1) | async-done | bytes 399392 | tf_op jit(solution)/shard_map/all_to_all | solution.py:38
  66.6 43.9 %while.12 = (s32[]{:T(128)}, f32[12,32,512]{2,1,0:T(8,128)S(1)}, f32[12,1,512]{2,1,0:T(1,128)S(1)}, f32[12,512]{1,0:T(8,128)S(1)}, f32[3072]{0:T(1024)S(1)}, /*i...) while((s32[]{:T(128)}, f32[12,32,512]{2,1,0:T(8,128)S(1)}, ...), condition=%wide.region_3.4_spmd, body=%wide.region_2.3_spmd.sunk | while | flops 213909504 | bytes 9961589 | solution.py:111
  66.6 1.7 exponential_convert_fusion.2
  70.2 1.7 exponential_convert_fusion.2
  73.9 1.7 exponential_convert_fusion.2
  77.5 1.7 exponential_convert_fusion.2
  81.2 1.7 exponential_convert_fusion.2
  84.9 1.7 exponential_convert_fusion.2
  88.5 1.7 exponential_convert_fusion.2
  92.2 1.7 exponential_convert_fusion.2
  95.8 1.7 exponential_convert_fusion.2
  99.5 1.7 exponential_convert_fusion.2
  103.1 1.7 exponential_convert_fusion.2
  106.8 1.7 exponential_convert_fusion.2
  111.7 1.7 copy.47
  113.4 8.5 %all-to-all-start.2 = ((f32[32,33,192]{2,1,0:T(8,128)}), f32[32,33,192]{2,1,0:T(8,128)S(1)}, u32[]{:S(2)}, u32[]{:S(2)}) async-start(f32[32,33,192]{2,1,0:T(8,128)} %copy.47), calls=%async_computation.2 | async-start | bytes 2621440 | tf_op jit(solution)/shard_map/all_to_all | solution.py:55
  122.2 19.6 %all-to-all-done.2 = f32[32,33,192]{2,1,0:T(8,128)S(1)} async-done(((f32[32,33,192]{2,1,0:T(8,128)}), f32[32,33,192]{2,1,0:T(8,128)S(1)}, u32[]{:S(2)}, u32[]{:S(2)}) %all-to-all-start.2) | async-done | bytes 811040 | tf_op jit(solution)/shard_map/all_to_all | solution.py:55
  142.7 32.9 %all_to_all.27 = f32[32,1,3072]{2,1,0:T(1,128)S(1)} all-to-all(f32[32,1,3072]{2,1,0:T(1,128)S(1)} %broadcast_in_dim.40), channel_id=1, replica_groups=mesh['row_0'=4,'row_1'=4,'row_2'=2,'col'=16] {'row_2','col'}, dimensions={0} | all-to-all | bytes 786432 | tf_op jit(solution)/shard_map/all_to_all | solution.py:15
  175.9 10.9 %all_to_all.28 = f32[16,1,3072]{2,1,0:T(1,128)S(1)} all-to-all(f32[16,1,3072]{2,1,0:T(1,128)S(1)} %broadcast_in_dim.41), channel_id=1, replica_groups=mesh['row_0'=4,'row_1'=4,'row_2'=2,'col'=16] {'row_0','row_1'}, dimensions={0} | all-to-all | bytes 393216 | tf_op jit(solution)/shard_map/all_to_all | solution.py:15
  188.1 2.9 %cholesky.16 = f32[32,32]{1,0:T(8,128)S(1)} custom-call(f32[32,32]{1,0:T(8,128)S(1)} %fusion.11), custom_call_target="Cholesky" | custom-call | tf_op jit(solution)/shard_map/jit(cholesky)/cholesky | solution.py:162
  192.4 2.4 %custom-call.7 = f32[1,32,32]{1,2,0:T(8,128)S(1)} custom-call(f32[1,32,32]{2,1,0:T(8,128)S(1)} %fusion.9), custom_call_target="InvertDiagBlocksLowerTriangular" | custom-call | tf_op jit(solution)/shard_map/jit(_solve_triangular)/triangular_solve | solution.py:163
  (90 shorter events, 36.9 us)
Async XLA Ops:
  1.6 22.2 %all-to-all-start = ((bf16[32,32,192]{2,1,0:T(8,128)(2,1)}), bf16[32,32,192]{2,1,0:T(8,128)(2,1)S(1)}, u32[]{:S(2)}, u32[]{:S(2)}) async-start(bf16[32,32,192]{2,1,0:T(8,128)(2,1)} %broadcast_in_dim.23), calls=%async_computation | async-start | bytes 1048576 | tf_op jit(solution)/shard_map/all_to_all | solution.py:15
  24.6 41.1 %all-to-all-start.1 = ((bf16[16,192,65]{1,2,0:T(8,128)(2,1)}), bf16[16,192,65]{1,2,0:T(8,128)(2,1)S(1)}, u32[]{:S(2)}, u32[]{:S(2)}) async-start(bf16[16,192,65]{1,2,0:T(8,128)(2,1)} %stack.2), calls=%async_computation.1 | async-start | bytes 1179648 | tf_op jit(solution)/shard_map/all_to_all | solution.py:38
  111.6 10.4 %copy-start = (f32[32,192]{1,0:T(8,128)S(1)}, f32[32,192]{1,0:T(8,128)}, u32[]{:S(2)}) copy-start(f32[32,192]{1,0:T(8,128)} %param.7) | copy-start | bytes 73732
  113.4 28.4 %all-to-all-start.2 = ((f32[32,33,192]{2,1,0:T(8,128)}), f32[32,33,192]{2,1,0:T(8,128)S(1)}, u32[]{:S(2)}, u32[]{:S(2)}) async-start(f32[32,33,192]{2,1,0:T(8,128)} %copy.47), calls=%async_computation.2 | async-start | bytes 2621440 | tf_op jit(solution)/shard_map/all_to_all | solution.py:55
